TPU v7x, 256 devices: a whole 4x4x8 slice. The times are simulated.
256 devices in a mesh: segment: 16 (over x, y), mp: 16 (over z, core).
Axes of the slice: x: 4, y: 4, z: 8, core: 2. Of those that a mesh axis runs over, the one named last changes fastest.
Arguments:
- noise_init: float32 [8192, 64], P('segment'), may hold values from -6 to 6
- step_noise: float32 [4, 8192, 64], P(None, 'segment'), may hold values from -6 to 6
- assign: int32 [128], P('segment'), may hold values from 0 to 31
- slot_map: int32 [128], replicated, may hold values from 0 to 255, as said below
- prompt_embed: bfloat16 [32, 1536], P('segment', 'mp'), may hold values from -6 to 6
- time_vec: bfloat16 [1536], P('mp'), may hold values from -6 to 6
- w_in: bfloat16 [64, 1536], P('segment', 'mp'), may hold values from -0.75 to 0.75
- ln_gain: bfloat16 [1536], P('mp'), may hold values from 0.099609375 to 1.8984375
- w_up: bfloat16 [1536, 6144], P('segment', 'mp'), may hold values from -0.15625 to 0.15625
- w_down: bfloat16 [6144, 1536], P('mp', 'segment'), may hold values from -0.109375 to 0.109375
- w_out: bfloat16 [1536, 64], P('mp', 'segment'), may hold values from -0.15625 to 0.15625
- conv_in_w: bfloat16 [3, 3, 16, 512], replicated, may hold values from -0.5 to 0.5
- gn_gain: float32 [512], replicated, may hold values from 0.1 to 1.9
- conv_mid_w: bfloat16 [3, 3, 512, 512], replicated, may hold values from -0.09375 to 0.09375
Outputs:
- latents: float32 [8192, 64], P('segment')
- decoded: bfloat16 [256, 2, 128, 512], P('segment', None, 'mp')
Inputs may be any that keep to these rules, and one draw needn't show every extreme that they name: `slot_map`: different samples have different slots. Decoder section d owns slots d * 16 to (d + 1) * 16 - 1; in every draw some section has all of its 16 slots filled, and slots 0 and 255 are used.
All inputs are finite; a program needn't handle non-finite values.
Results may differ from a plain program's by a relative error of at most 0.015.
Values may be sent and summed in bfloat16 or wider, within the bound.
A program may use at most 64 MiB of HBM per device.

v0:
```python
import math

import jax
import jax.numpy as jnp
from jax import lax
from jax.sharding import PartitionSpec as P

LAT_CH = 16
VC = 512
GROUPS = 32
STEPS = 4


NOISE_SCALE = 0.5
LATENT_SCALE = 1.0 / 1.5305
EPSILON = 1e-06


def split_up(value, dim, devices):
    before, after = (value.shape[:dim], value.shape[dim + 1 :])
    return jnp.moveaxis(value.reshape(*before, devices, -1, *after), dim, 0)


def sum_at_owner(value, axis, dim):
    blocks = split_up(value, dim, lax.axis_size(axis))
    arrived = lax.all_to_all(blocks, axis, split_axis=0, concat_axis=0, tiled=True)
    return arrived.astype(jnp.float32).sum(axis=0)


def sent_to_all(value, axis):
    copies = jnp.broadcast_to(value, (lax.axis_size(axis), *value.shape))
    return lax.all_to_all(copies, axis, split_axis=0, concat_axis=0, tiled=True)


def taken_together(value, axis):
    return sent_to_all(value, axis).astype(jnp.float32).sum(axis=0)


def joined_along(blocks, dim):
    blocks = jnp.moveaxis(blocks, 0, dim)
    lengths = blocks.shape
    return blocks.reshape(*lengths[:dim], lengths[dim] * lengths[dim + 1], *lengths[dim + 2 :])


def gathered_copies(value, axis, dim):
    return joined_along(sent_to_all(value, axis), dim)


def conv_rows(padded, weight, col_count):
    accumulated = None
    for row_shift in range(3):
        for col_shift in range(3):
            window = padded[:, row_shift : row_shift + 2, col_shift : col_shift + col_count, :]
            product = jnp.einsum(
                "nrcv,vw->nrcw",
                window,
                weight[row_shift, col_shift],
                preferred_element_type=jnp.float32,
            )
            accumulated = product if accumulated is None else accumulated + product
    return accumulated


def decode_tile(latent_tile, mp_index, tile_cols, image_cols, conv_in_w, gn_gain, conv_mid_w):
    slot_rows = latent_tile.shape[0]
    padded = jnp.pad(latent_tile.astype(jnp.bfloat16), ((0, 0), (1, 1), (0, 0), (0, 0)))
    first_wide = conv_rows(padded, conv_in_w, tile_cols + 2)
    conv_first = first_wide[:, :, 1 : tile_cols + 1, :]
    per_group = VC // GROUPS
    grouped = conv_first.reshape(slot_rows, 2 * tile_cols, GROUPS, per_group)
    group_sum, group_square = lax.psum(
        (jnp.sum(grouped, axis=(1, 3)), jnp.sum(grouped * grouped, axis=(1, 3))), "mp"
    )
    entries = 2 * image_cols * per_group
    average = group_sum / entries
    variance = jnp.maximum(group_square / entries - average * average, 0.0)
    inv_spread = lax.rsqrt(variance + EPSILON)
    columns = mp_index * tile_cols - 1 + jnp.arange(tile_cols + 2, dtype=jnp.int32)
    inside = (columns >= 0) & (columns < image_cols)
    col_count = first_wide.shape[2]
    shaped = first_wide.reshape(slot_rows, 2, col_count, GROUPS, per_group)
    shaped = (shaped - average[:, None, None, :, None]) * inv_spread[:, None, None, :, None]
    act_wide = jnp.where(
        inside[None, None, :, None],
        jax.nn.silu(shaped.reshape(slot_rows, 2, col_count, VC) * gn_gain),
        0.0,
    ).astype(jnp.bfloat16)
    act_padded = jnp.pad(act_wide, ((0, 0), (1, 1), (0, 0), (0, 0)))
    return (conv_first + conv_rows(act_padded, conv_mid_w, tile_cols)).astype(jnp.bfloat16)


def full_front(
    latent_state,
    w_in_full,
    prompt_cond,
    time_full,
    gain_full,
    time_now,
    samples_here,
    tok_sample,
    tok_group,
):
    embedded = jnp.dot(
        latent_state.astype(jnp.bfloat16), w_in_full, preferred_element_type=jnp.float32
    )
    hidden_in = (embedded.reshape(samples_here, tok_sample, -1) + prompt_cond[:, None, :]).reshape(
        tok_group, -1
    ) + time_now * time_full.astype(jnp.float32)
    average = jnp.mean(hidden_in, axis=-1, keepdims=True)
    centered = hidden_in - average
    variance = jnp.mean(centered * centered, axis=-1, keepdims=True)
    normed = (centered * lax.rsqrt(variance + EPSILON) * gain_full.astype(jnp.float32)).astype(
        jnp.bfloat16
    )
    return (hidden_in, normed)


def per_device(
    noise_init,
    step_noise,
    assign,
    slot_map,
    prompt_embed,
    time_vec,
    w_in,
    ln_gain,
    w_up,
    w_down,
    w_out,
    conv_in_w,
    gn_gain,
    conv_mid_w,
):
    mp_count = lax.axis_size("mp")
    mp_index = lax.axis_index("mp")
    segment_index = lax.axis_index("segment")
    w_in_rows, w_up_rows, w_down_cols, w_out_cols, prompt_rows = (
        lax.all_gather(w_in, "segment", axis=0, tiled=True),
        lax.all_gather(w_up, "segment", axis=0, tiled=True),
        lax.all_gather(w_down, "segment", axis=1, tiled=True),
        lax.all_gather(w_out, "segment", axis=1, tiled=True),
        lax.all_gather(prompt_embed, "segment", axis=0, tiled=True),
    )
    samples_here = assign.shape[0]
    tok_group = noise_init.shape[0]
    tok_sample = tok_group // samples_here
    prompt_count = prompt_rows.shape[0]
    choose = (assign[:, None] == jnp.arange(prompt_count, dtype=jnp.int32)[None, :]).astype(
        jnp.bfloat16
    )
    step_size = 1.0 / STEPS
    noise_gain = NOISE_SCALE * math.sqrt(step_size)
    latent_state = noise_init
    w_in_full, prompt_full, time_full, gain_full = (
        lax.all_gather(w_in_rows, "mp", axis=1, tiled=True),
        lax.all_gather(prompt_rows, "mp", axis=1, tiled=True),
        lax.all_gather(time_vec, "mp", axis=0, tiled=True),
        lax.all_gather(ln_gain, "mp", axis=0, tiled=True),
    )
    prompt_cond = jnp.dot(choose, prompt_full, preferred_element_type=jnp.float32)
    feat_width = w_out_cols.shape[0]
    for step_index in range(STEPS):
        time_now = 1.0 - step_index * step_size
        hidden_in, normed = full_front(
            latent_state,
            w_in_full,
            prompt_cond,
            time_full,
            gain_full,
            time_now,
            samples_here,
            tok_sample,
            tok_group,
        )
        act = jax.nn.gelu(
            jnp.dot(normed, w_up_rows, preferred_element_type=jnp.float32), approximate=True
        ).astype(jnp.bfloat16)
        mlp_share = sum_at_owner(
            jnp.dot(act, w_down_cols, preferred_element_type=jnp.float32).astype(jnp.bfloat16),
            "mp",
            1,
        )
        hidden_part = lax.dynamic_slice_in_dim(hidden_in, mp_index * feat_width, feat_width, 1)
        partial_vel = jnp.dot(
            (hidden_part + mlp_share).astype(jnp.bfloat16),
            w_out_cols,
            preferred_element_type=jnp.float32,
        )
        velocity = taken_together(partial_vel.astype(jnp.bfloat16), "mp").astype(jnp.float32)
        latent_state = latent_state - step_size * velocity + noise_gain * step_noise[step_index]
    image_cols = 2 * tok_sample
    tile_cols = image_cols // mp_count
    images = (
        latent_state.reshape(samples_here, tok_sample, 2, 2, LAT_CH)
        .transpose(0, 2, 1, 3, 4)
        .reshape(samples_here, 2, image_cols, LAT_CH)
        * LATENT_SCALE
    )
    widened = jnp.pad(images, ((0, 0), (0, 0), (2, 2), (0, 0)))
    latent_tile = lax.dynamic_slice_in_dim(widened, mp_index * tile_cols, tile_cols + 4, 2)
    slot_count = 2 * samples_here
    first_slot = segment_index * slot_count
    slot_ids = first_slot + jnp.arange(slot_count, dtype=jnp.int32)
    own_feats = decode_tile(
        latent_tile, mp_index, tile_cols, image_cols, conv_in_w, gn_gain, conv_mid_w
    )
    slot_picks = (slot_map[None, :] == slot_ids[:, None]).astype(jnp.bfloat16)
    flat_feats = own_feats.reshape(samples_here, -1)
    placed = jnp.dot(
        slot_picks, gathered_copies(flat_feats, "segment", 0), preferred_element_type=jnp.float32
    )
    decoded = placed.astype(jnp.bfloat16).reshape(slot_count, 2, tile_cols, VC)
    return (latent_state, decoded)


def solution(mesh):
    return jax.shard_map(
        per_device,
        mesh=mesh,
        in_specs=(
            P("segment", None),
            P(None, "segment", None),
            P("segment"),
            P(),
            P("segment", "mp"),
            P("mp"),
            P("segment", "mp"),
            P("mp"),
            P("segment", "mp"),
            P("mp", "segment"),
            P("mp", "segment"),
            P(),
            P(),
            P(),
        ),
        out_specs=(P("segment", None), P("segment", None, "mp", None)),
        check_vma=False,
    )
```

profile of v0, /device:TPU:1, one launch (start us, length us, event | category | flops | bytes accessed | tf_op | source)
XLA Modules:
  0.0 552.0 jit_solution(1239499764776693210)
XLA Ops:
  7.9 0.7 all-gather.8.cloned.1.call-update
  8.7 1.3 dynamic-slice
  10.6 0.9 dynamic-update-slice
  11.4 0.8 dynamic-update-slice.1
  12.3 27.9 %all-reduce.6 = (bf16[1536]{0:T(1024)(128)(2,1)S(1)}, bf16[1536]{0:T(1024)(128)(2,1)S(1)}) all-reduce(bf16[1536]{0:T(1024)(128)(2,1)S(1)} %dynamic-update-slice, bf16[1536]{0:T(1024)(128)(2,1)S(1)} %dynamic-update-slice.1), channel_id=1, replica_groups=mesh['segment'=16,'mp'=16] {'mp'}, use_global_device_ids=true, to_apply=%add.3 | all-reduce | flops 3072 | bytes 12288
  40.2 19.3 %all-gather = bf16[16,4,96]{2,1,0:T(4,128)(2,1)S(1)} all-gather(bf16[1,4,96]{2,1,0:T(4,128)(2,1)} %bitcast.242), channel_id=1, replica_groups=mesh['segment'=16,'mp'=16] {'segment'}, dimensions={0}, use_global_device_ids=true | all-gather | bytes 13056 | tf_op jit(solution)/shard_map/all_gather | solution.py:138
  59.5 22.0 %all-gather.1 = bf16[16,96,64]{1,2,0:T(8,128)(2,1)S(1)} all-gather(bf16[1,96,64]{1,2,0:T(8,128)(2,1)S(1)} %bitcast.240), channel_id=1, replica_groups=mesh['segment'=16,'mp'=16] {'mp'}, dimensions={0}, use_global_device_ids=true | all-gather | bytes 208896 | tf_op jit(solution)/shard_map/all_gather | solution.py:155
  81.9 15.8 %all-gather.2 = bf16[16,2,96]{2,1,0:T(2,128)(2,1)S(1)} all-gather(bf16[1,2,96]{2,1,0:T(2,128)(2,1)} %bitcast.244), channel_id=1, replica_groups=mesh['segment'=16,'mp'=16] {'segment'}, dimensions={0}, use_global_device_ids=true | all-gather | bytes 6528 | tf_op jit(solution)/shard_map/all_gather | solution.py:142
  97.7 20.3 %all-gather.3 = bf16[16,96,32]{1,2,0:T(8,128)(2,1)S(1)} all-gather(bf16[1,96,32]{1,2,0:T(8,128)(2,1)S(1)} %bitcast.241), channel_id=1, replica_groups=mesh['segment'=16,'mp'=16] {'mp'}, dimensions={0}, use_global_device_ids=true | all-gather | bytes 104448 | tf_op jit(solution)/shard_map/all_gather | solution.py:156
  118.2 0.8 fusion.124
  119.1 1.6 fusion.158
  121.2 4.8 convolution_convert_fusion.4
  125.9 2.6 copy.43
  128.6 4.3 all-to-all-start
  132.9 17.3 %all-gather.4 = bf16[16,4,96]{2,1,0:T(4,128)(2,1)S(1)} all-gather(bf16[1,4,96]{2,1,0:T(4,128)(2,1)S(1)} %bitcast.243), channel_id=1, replica_groups=mesh['segment'=16,'mp'=16] {'segment'}, dimensions={0}, use_global_device_ids=true | all-gather | bytes 13056 | tf_op jit(solution)/shard_map/all_gather | solution.py:141
  150.2 21.2 %all-to-all-done = bf16[16,512,96]{1,2,0:T(8,128)(2,1)} async-done(((bf16[16,512,96]{1,2,0:T(8,128)(2,1)}), bf16[16,512,96]{1,2,0:T(8,128)(2,1)}, u32[]{:S(2)}, u32[]{:S(2)}) %all-to-all-start) | async-done | bytes 1572896 | tf_op jit(solution)/shard_map/all_to_all | solution.py:26
  171.4 2.3 convert_reduce_fusion.3
  173.7 1.8 copy.44
  175.5 1.2 convolution_convert_fusion.8
  176.8 1.1 broadcast_in_dim.18
  177.9 4.3 all-to-all-start.1
  182.1 1.3 convert_multiply_fusion.1
  183.4 26.6 %all-to-all-done.1 = bf16[16,512,64]{1,2,0:T(8,128)(2,1)S(1)} async-done(((bf16[16,512,64]{1,2,0:T(8,128)(2,1)}), bf16[16,512,64]{1,2,0:T(8,128)(2,1)S(1)}, u32[]{:S(2)}, u32[]{:S(2)}) %all-to-all-start.1) | async-done | bytes 1048608 | tf_op jit(solution)/shard_map/all_to_all | solution.py:32
  210.2 1.6 fusion.159
  212.6 4.7 convolution_convert_fusion.3
  217.3 2.6 copy.45
  219.9 43.3 %all_to_all.45 = bf16[16,512,96]{1,2,0:T(8,128)(2,1)S(1)} all-to-all(bf16[16,512,96]{1,2,0:T(8,128)(2,1)} %bitcast.229), channel_id=1, replica_groups=mesh['segment'=16,'mp'=16] {'mp'}, dimensions={0} | all-to-all | bytes 3145728 | tf_op jit(solution)/shard_map/all_to_all | solution.py:26
  263.2 0.9 convert_reduce_fusion.2
  264.1 1.8 copy.46
  265.9 1.3 convolution_convert_fusion.7
  267.3 31.3 %all_to_all.46 = bf16[16,512,64]{1,2,0:T(8,128)(2,1)S(1)} all-to-all(bf16[16,512,64]{1,2,0:T(8,128)(2,1)S(1)} %broadcast_in_dim.19), channel_id=1, replica_groups=mesh['segment'=16,'mp'=16] {'mp'}, dimensions={0} | all-to-all | bytes 2097152 | tf_op jit(solution)/shard_map/all_to_all | solution.py:32
  298.8 0.7 fusion.160
  299.9 4.8 convolution_convert_fusion.2
  304.7 2.6 copy.47
  307.3 42.7 %all_to_all.47 = bf16[16,512,96]{1,2,0:T(8,128)(2,1)S(1)} all-to-all(bf16[16,512,96]{1,2,0:T(8,128)(2,1)} %bitcast.230), channel_id=1, replica_groups=mesh['segment'=16,'mp'=16] {'mp'}, dimensions={0} | all-to-all | bytes 3145728 | tf_op jit(solution)/shard_map/all_to_all | solution.py:26
  350.0 0.9 convert_reduce_fusion.1
  350.9 1.8 copy.48
  352.6 1.2 convolution_convert_fusion.6
  354.0 31.3 %all_to_all.48 = bf16[16,512,64]{1,2,0:T(8,128)(2,1)S(1)} all-to-all(bf16[16,512,64]{1,2,0:T(8,128)(2,1)S(1)} %broadcast_in_dim.20), channel_id=1, replica_groups=mesh['segment'=16,'mp'=16] {'mp'}, dimensions={0} | all-to-all | bytes 2097152 | tf_op jit(solution)/shard_map/all_to_all | solution.py:32
  385.4 1.6 fusion.161
  387.5 4.8 convolution_convert_fusion.1
  392.3 2.6 copy.49
  394.9 42.7 %all_to_all.49 = bf16[16,512,96]{1,2,0:T(8,128)(2,1)S(1)} all-to-all(bf16[16,512,96]{1,2,0:T(8,128)(2,1)} %bitcast.231), channel_id=1, replica_groups=mesh['segment'=16,'mp'=16] {'mp'}, dimensions={0} | all-to-all | bytes 3145728 | tf_op jit(solution)/shard_map/all_to_all | solution.py:26
  437.6 0.9 convert_reduce_fusion
  438.5 1.8 copy.50
  440.3 1.2 convolution_convert_fusion.5
  441.5 1.1 broadcast_in_dim.21
  442.6 3.5 all-to-all-start.7
  446.2 27.3 %all-to-all-done.7 = bf16[16,512,64]{1,2,0:T(8,128)(2,1)S(1)} async-done(((bf16[16,512,64]{1,2,0:T(8,128)(2,1)}), bf16[16,512,64]{1,2,0:T(8,128)(2,1)S(1)}, u32[]{:S(2)}, u32[]{:S(2)}) %all-to-all-start.7) | async-done | bytes 1048608 | tf_op jit(solution)/shard_map/all_to_all | solution.py:32
  473.6 0.7 broadcast_multiply_fusion
  477.3 22.2 %all-reduce.5 = (f32[8,32]{1,0:T(8,128)S(1)}, f32[8,32]{1,0:T(8,128)S(1)}) all-reduce(f32[8,32]{1,0:T(8,128)S(1)} %reduce_sum.197, f32[8,32]{1,0:T(8,128)S(1)} %reduce_sum.194), channel_id=1, replica_groups=mesh['segment'=16,'mp'=16] {'mp'}, use_global_device_ids=true, to_apply=%region_21.22 | all-reduce | flops 512 | bytes 4096 | tf_op jit(solution)/shard_map/psum | solution.py:71
  500.1 1.3 fusion.64
  501.4 1.3 convolution_add_fusion.15
  502.7 1.3 convolution_add_fusion.14
  504.0 1.3 convolution_add_fusion.13
  505.3 1.3 convolution_add_fusion.12
  506.6 1.3 convolution_add_fusion.11
  507.9 1.3 convolution_add_fusion.10
  509.2 1.3 convolution_add_fusion.9
  510.4 1.3 fusion.23
  511.8 1.6 broadcast_in_dim.24
  513.4 5.2 all-to-all-start.8
  518.7 25.3 %all-to-all-done.8 = bf16[16,8,8192]{2,1,0:T(8,128)(2,1)S(1)} async-done(((bf16[16,8,8192]{2,1,0:T(8,128)(2,1)}), bf16[16,8,8192]{2,1,0:T(8,128)(2,1)S(1)}, u32[]{:S(2)}, u32[]{:S(2)}) %all-to-all-start.8) | async-done | bytes 2097184 | tf_op jit(solution)/shard_map/all_to_all | solution.py:32
  544.4 0.8 copy.71
  (91 shorter events, 8.4 us)
Async XLA Ops:
  7.2 114.0 %all-gather.10.cloned.1.call-start = ((), (), s32[]{:S(2)}) async-start(), calls=%async_computation.10 | async-start | bytes 1253376 | tf_op jit(solution)/shard_map/all_gather | solution.py:140
  7.9 113.3 %all-gather.8.cloned.1.call-start = ((), (), s32[]{:S(2)}) async-start(), calls=%async_computation.9 | async-start | bytes 1253376 | tf_op jit(solution)/shard_map/all_gather | solution.py:139
  40.2 19.3 %copy-start.9 = (bf16[1536]{0:T(1024)(128)(2,1)}, bf16[1536]{0:T(1024)(128)(2,1)S(1)}, u32[]{:S(2)}) copy-start(bf16[1536]{0:T(1024)(128)(2,1)S(1)} %get-tuple-element.6) | copy-start | bytes 9220
  118.2 3.0 copy-start.10
  125.9 6.9 %copy-start.14 = (bf16[96,4]{0,1:T(4,128)(2,1)S(1)}, bf16[96,4]{0,1:T(4,128)(2,1)}, u32[]{:S(2)}) copy-start(bf16[96,4]{0,1:T(4,128)(2,1)} %param.24) | copy-start | bytes 2308
  128.6 42.9 %all-to-all-start = ((bf16[16,512,96]{1,2,0:T(8,128)(2,1)}), bf16[16,512,96]{1,2,0:T(8,128)(2,1)}, u32[]{:S(2)}, u32[]{:S(2)}) async-start(bf16[16,512,96]{1,2,0:T(8,128)(2,1)} %bitcast.228), calls=%async_computation | async-start | bytes 3145728 | tf_op jit(solution)/shard_map/all_to_all | solution.py:26
  173.7 36.5 %copy-start.2 = (f32[512,64]{0,1:T(8,128)S(1)}, f32[512,64]{0,1:T(8,128)}, u32[]{:S(2)}) copy-start(f32[512,64]{0,1:T(8,128)} %param.14) | copy-start | bytes 393220
  177.9 32.2 %all-to-all-start.1 = ((bf16[16,512,64]{1,2,0:T(8,128)(2,1)}), bf16[16,512,64]{1,2,0:T(8,128)(2,1)S(1)}, u32[]{:S(2)}, u32[]{:S(2)}) async-start(bf16[16,512,64]{1,2,0:T(8,128)(2,1)} %broadcast_in_dim.18), calls=%async_computation.1 | async-start | bytes 2097152 | tf_op jit(solution)/shard_map/all_to_all | solution.py:32
  210.2 1.7 copy-start.6
  211.9 0.7 copy-start.11
  265.9 32.8 %copy-start = (f32[4,512,64]{1,2,0:T(8,128)S(1)}, f32[4,512,64]{1,2,0:T(8,128)}, u32[]{:S(2)}) copy-start(f32[4,512,64]{1,2,0:T(8,128)} %param.15) | copy-start | bytes 1572868
  265.9 32.8 %copy-start.3 = (f32[512,64]{0,1:T(8,128)S(1)}, f32[512,64]{0,1:T(8,128)}, u32[]{:S(2)}) copy-start(f32[512,64]{0,1:T(8,128)} %param.14) | copy-start | bytes 393220
  265.9 32.8 %copy-start.7 = (f32[512,64]{0,1:T(8,128)S(1)}, f32[512,64]{0,1:T(8,128)}, u32[]{:S(2)}) copy-start(f32[512,64]{0,1:T(8,128)} %copy-done.6) | copy-start | bytes 393220
  385.4 1.7 copy-start.4
  385.4 2.1 copy-start.12
  438.5 35.1 %copy-start.5 = (f32[512,64]{0,1:T(8,128)S(1)}, f32[512,64]{0,1:T(8,128)}, u32[]{:S(2)}) copy-start(f32[512,64]{0,1:T(8,128)} %copy-done.4) | copy-start | bytes 393220
  441.5 32.1 %copy-start.1 = (f32[4,512,64]{1,2,0:T(8,128)S(1)}, f32[4,512,64]{1,2,0:T(8,128)}, u32[]{:S(2)}) copy-start(f32[4,512,64]{1,2,0:T(8,128)} %param.15) | copy-start | bytes 1572868
  441.5 33.5 %copy-start.8 = (bf16[3,3,16,512]{3,2,1,0:T(8,128)(2,1)S(1)}, bf16[3,3,16,512]{3,2,1,0:T(8,128)(2,1)}, u32[]{:S(2)}) copy-start(bf16[3,3,16,512]{3,2,1,0:T(8,128)(2,1)} %param.25) | copy-start | bytes 442372
  442.6 30.8 %all-to-all-start.7 = ((bf16[16,512,64]{1,2,0:T(8,128)(2,1)}), bf16[16,512,64]{1,2,0:T(8,128)(2,1)S(1)}, u32[]{:S(2)}, u32[]{:S(2)}) async-start(bf16[16,512,64]{1,2,0:T(8,128)(2,1)} %broadcast_in_dim.21), calls=%async_computation.7 | async-start | bytes 2097152 | tf_op jit(solution)/shard_map/all_to_all | solution.py:32
  476.0 24.0 %copy-start.13 = (f32[512]{0:T(512)S(1)}, f32[512]{0:T(512)}, u32[]{:S(2)}) copy-start(f32[512]{0:T(512)} %param.26) | copy-start | bytes 6148
  511.8 32.1 %copy-start.15 = (s32[128]{0:T(128)S(1)}, s32[128]{0:T(128)}, u32[]{:S(2)}) copy-start(s32[128]{0:T(128)} %param.17) | copy-start | bytes 1540
  513.4 30.5 %all-to-all-start.8 = ((bf16[16,8,8192]{2,1,0:T(8,128)(2,1)}), bf16[16,8,8192]{2,1,0:T(8,128)(2,1)S(1)}, u32[]{:S(2)}, u32[]{:S(2)}) async-start(bf16[16,8,8192]{2,1,0:T(8,128)(2,1)} %broadcast_in_dim.24), calls=%async_computation.8 | async-start | bytes 4194304 | tf_op jit(solution)/shard_map/all_to_all | solution.py:32
Sparse Core Ops, SparseCore 0:
  10.5 51.0 all-gather.9
  64.0 47.5 all-gather.7
where the time goes:
time: 557 us; the launch traced here: 552 us
  blocking collectives  336 us (60%)
  waiting for transfers between devices  102 us (18%)
  matrix products  44.1 us (8%)
  local copies, waits for them, and re-layouts  27.4 us (5%)
  starting transfers between devices  17.4 us (3%)
  between operations  15.3 us (3%)
  other arithmetic  10 us (2%)
    all_to_all x3, blocking collectives, sum_at_owner(): lax.all_to_all(blocks, axis, split_axis=0, concat_axis=0, tiled=True)  129 us
    all_to_all x3, waiting for transfers between devices, sent_to_all(): return lax.all_to_all(copies, axis, split_axis=0, concat_axis=0, tiled=True)  79.2 us
    all_to_all x2, blocking collectives, sent_to_all(): return lax.all_to_all(copies, axis, split_axis=0, concat_axis=0, tiled=True)  62.5 us
    unnamed x1, blocking collectives  27.9 us
    psum x1, blocking collectives, decode_tile(): lax.psum((jnp.sum(grouped, axis=(1, 3)), jnp.sum(grouped * grouped, axis=...  22.2 us
    all_gather x1, blocking collectives, per_device(): lax.all_gather(w_in_rows, 'mp', axis=1, tiled=True)  22 us
    all_to_all x1, waiting for transfers between devices, sum_at_owner(): lax.all_to_all(blocks, axis, split_axis=0, concat_axis=0, tiled=True)  21.2 us
    all_gather x1, blocking collectives, per_device(): lax.all_gather(prompt_rows, 'mp', axis=1, tiled=True)  20.3 us
  transfers between devices with their start and end apart: 6, of which 4 were waited for; matrix products, arithmetic and copies ran while one was open for 1% of the time, Pallas kernels for 0%

commit v1 on v0

v1 whole, which is shorter than its diff:
```python
import jax
import jax.numpy as jnp
from jax import lax
from jax.experimental import pallas as pl
from jax.experimental.pallas import tpu as pltpu
from jax.sharding import PartitionSpec as P

MESH = pl.DeviceIdType.MESH
F32, BF16 = jnp.float32, jnp.bfloat16
HIGH = lax.Precision.HIGHEST
D, FF, VC, GROUPS, STEPS = 1536, 6144, 512, 32, 4
EPSILON = 1e-6
LATENT_SCALE = 1.0 / 1.5305
STEP = 1.0 / STEPS
NOISE_GAIN = 0.5 * STEP**0.5
TIME_ROW, ONES_ROW, GAIN_ROW = 160, 161, 162
Z_ORDER = (1, 7, 2, 6, 3, 5, 4)


def dot(a, b, **kw):
    return jnp.dot(a, b, preferred_element_type=F32, **kw)


def dot_t(a, b):
    return lax.dot_general(a, b, (((1,), (1,)), ((), ())), preferred_element_type=F32)


def iota(shape, dim):
    return lax.broadcasted_iota(jnp.int32, shape, dim)


def onehot(mask):
    return jnp.where(mask, 1.0, 0.0).astype(BF16)


def split(value):
    high = value.astype(BF16)
    return high, (value - high.astype(F32)).astype(BF16)


def kernel(
    assign, slot_map, noise0, noise_k, prompt, time_vec, w_in, gain, w_up, w_down, w_out, conv_in, gn_gain, conv_mid,
    lat_ref, dec_ref,
    piece, tables, gram, part, parts, chunks, gy_own, gy_z, gy_all, vel_out, vel_in, state,
    tile_out, tile_z, tile_pack, tiles, lat_out, lat_in, noise_a, noise_b, w_mid, w_tok, act0, act1,
    in_sem, send_p, recv_p, send_r, recv_r, send_z, recv_z, send_g, recv_g, send_c, recv_c, send_h, recv_h,
    send_v, recv_v, send_t, recv_t, send_u, recv_u, send_l, recv_l,
):
    s, m = lax.axis_index("segment"), lax.axis_index("mp")
    z, c = lax.div(m, 2), lax.rem(m, 2)
    on_diagonal = m == s

    def remote(src, dst, ssem, rsem, device):
        return pltpu.make_async_remote_copy(
            src_ref=src, dst_ref=dst, send_sem=ssem, recv_sem=rsem, device_id=device, device_id_type=MESH
        )

    def plane(i):
        return lax.rem(s + i, 16), m

    def along_z(i):
        return s, lax.rem(z + i, 8) * 2 + c

    other_core = (s, m + 1 - 2 * c)

    def drain(ref, sem):
        pltpu.make_async_copy(ref, ref, sem).wait()

    barrier = pltpu.get_barrier_semaphore()

    def greet(device):
        pl.semaphore_signal(barrier, inc=1, device_id=device, device_id_type=MESH)

    @pl.loop(0, 16)
    def _(i):
        @pl.when(jnp.logical_not(jnp.logical_and(on_diagonal, i == s)))
        def _():
            greet((i, s))

    @pl.loop(1, 16)
    def _(i):
        greet(plane(i))

    @pl.loop(1, 8)
    def _(i):
        greet(along_z(i))

    greet(other_core)

    rows = pl.ds(pl.multiple_of(z * 64, 64), 64)
    in_noise = pltpu.make_async_copy(noise0.at[rows], noise_a, in_sem.at[0])
    in_steps = pltpu.make_async_copy(noise_k.at[:, rows], noise_b, in_sem.at[1])
    in_mid = pltpu.make_async_copy(conv_mid, w_mid, in_sem.at[2])
    in_noise.start()
    in_steps.start()
    in_mid.start()

    first = jnp.where(s == 0, 1.0, 0.0)
    turned = dot_t(onehot(iota((4, 4), 0) == iota((4, 4), 1)), w_out[...])
    block = jnp.concatenate(
        [
            w_in[...].astype(F32),
            prompt[...].astype(F32),
            time_vec[...].astype(F32).reshape(1, 96) * first,
            jnp.ones((1, 96), F32),
            turned,
            gain[...].astype(F32).reshape(1, 96),
            jnp.zeros((3, 96), F32),
        ],
        axis=0,
    )
    piece[...] = jnp.concatenate([block, jnp.zeros((16, 32), F32)], axis=1).astype(BF16)

    @pl.when(on_diagonal)
    def _():
        tables[s] = piece[...]

    pl.semaphore_wait(barrier, 39 - jnp.where(on_diagonal, 1, 0))

    def to_features(i):
        return remote(piece, tables.at[s], send_p, recv_p, (m, i))

    @pl.loop(0, 16)
    def _(i):
        @pl.when(jnp.logical_not(jnp.logical_and(on_diagonal, i == m)))
        def _():
            to_features(i).start()

    w_tok[...] = jnp.zeros(w_tok.shape, BF16)
    for row in range(2):
        for col in range(2):
            for src_row in range(2):
                for tap in range(3):
                    offset = col + tap - 1 + 2
                    to = (offset // 2) * 64 + (2 * src_row + offset % 2) * 16
                    at = (2 * row + col) * VC
                    w_tok[to : to + 16, at : at + VC] = conv_in[src_row - row + 1, tap]

    @pl.when(on_diagonal)
    def _():
        drain(tables.at[pl.ds(0, 15)], recv_p)

    @pl.when(jnp.logical_not(on_diagonal))
    def _():
        drain(tables, recv_p)

    want = iota((256, 256), 0)
    have = iota((256, 256), 1)
    prompt_row, out_row = want - 64, want - 96
    source = jnp.where(
        want < 64,
        (want >> 2) * 16 + (want & 3),
        jnp.where(
            want < 96,
            (prompt_row >> 1) * 16 + 4 + (prompt_row & 1),
            jnp.where(
                want < 160,
                (out_row >> 2) * 16 + 8 + (out_row & 3),
                jnp.where(want == TIME_ROW, 6, jnp.where(want == ONES_ROW, 7, jnp.where(want == GAIN_ROW, 12, -1))),
            ),
        ),
    )
    table = dot(onehot(source == have), tables[...].reshape(256, 128))
    table16 = table.astype(BF16)
    scaled_high, scaled_low = split(table * table[GAIN_ROW : GAIN_ROW + 1])
    up_part = dot(scaled_high[:, :96], w_up[...]) + dot(scaled_low[:, :96], w_up[...])
    down_part = dot_t(table16[96:160, :96], w_down[...])
    gram[...] = dot_t(table16, table16)
    for third in range(3):
        lanes = slice(128 * third, 128 * third + 128)
        for group in range(10):
            number = third * 10 + group
            to = (number % 2) * 16
            if group < 6:
                part[number // 2, to : to + 16] = up_part[16 * group : 16 * group + 16, lanes]
            else:
                part[number // 2, to : to + 16] = down_part[16 * group - 96 : 16 * group - 80, lanes]
    part[15, 0:32] = jnp.zeros((32, 128), F32)
    for third in range(3):
        lanes = slice(128 * third, 128 * third + 128)
        part[15, third : third + 1] = up_part[TIME_ROW : TIME_ROW + 1, lanes]
    gain_up = jnp.concatenate(
        [up_part[ONES_ROW : ONES_ROW + 1, 128 * third : 128 * third + 128] for third in range(3)], axis=0
    )
    sums = gram[ONES_ROW : ONES_ROW + 1]
    for owner in range(16):
        first_row = 8 * owner + (64 if owner >= 12 else 0)
        own = gram[pl.ds(first_row + z, 1)]
        part[owner, 32:40] = jnp.concatenate(
            [sums[:, :128], sums[:, 128:], gain_up, own[:, :128], own[:, 128:], jnp.zeros((1, 128), F32)], axis=0
        )

    def to_owner(i):
        target = lax.rem(s + i, 16)
        return remote(part.at[target], parts.at[s], send_r, recv_r, (target, m))

    @pl.loop(1, 16)
    def _(i):
        to_owner(i).start()

    parts[s] = part[s]
    drain(parts.at[pl.ds(0, 15)], recv_r)

    total = parts[0]
    for source_s in range(1, 16):
        total = total + parts[source_s]
    mean = jnp.concatenate([total[32:33], total[33:34]], axis=1) / D
    gain_rows = total[34:37]
    lane16 = iota((16, 256), 1)
    row16 = iota((16, 256), 0)
    mean_time = jnp.sum(jnp.where(iota((1, 256), 1) == TIME_ROW, mean, 0.0), axis=1, keepdims=True)
    for half in range(2):
        number = 2 * s + half
        third = lax.div(number, 10)
        group = lax.rem(number, 10)
        block = total[16 * half : 16 * half + 16]
        column = jnp.sum(jnp.where(lane16 == row16 + 16 * group, mean, 0.0), axis=1, keepdims=True)
        column = jnp.where(group < 6, column, 0.0)
        row = jnp.where(third == 0, gain_rows[0:1], jnp.where(third == 1, gain_rows[1:2], gain_rows[2:3]))
        if half == 0:
            time_rows = jnp.concatenate([mean_time * gain_rows, jnp.zeros((13, 128), F32)], axis=0)
        else:
            time_rows = jnp.zeros((16, 128), F32)
        taken = jnp.where(s == 15, time_rows, column * row)
        chunks[z, s, 16 * half : 16 * half + 16] = (block - taken).astype(BF16)
    own = jnp.concatenate([total[37:38], total[38:39]], axis=1)
    own_index = 8 * s + z
    own_lane = own_index + jnp.where(own_index >= 96, 64, 0)
    lane1 = iota((1, 256), 1)
    own_mean = jnp.sum(jnp.where(lane1 == own_lane, mean, 0.0), axis=1, keepdims=True)
    is_gram = jnp.logical_or(lane1 < 96, lane1 == TIME_ROW)
    own = jnp.where(is_gram, own / D - own_mean * mean, own)
    gy_own[...] = jnp.concatenate([own[:, :128], own[:, 128:], jnp.zeros((6, 128), F32)], axis=0)
    gy_z[z] = gy_own[...]

    def chunk_z(i):
        return remote(chunks.at[z, s], chunks.at[z, s], send_z, recv_z.at[i], along_z(i))

    def gram_z(i):
        return remote(gy_own, gy_z.at[z], send_g, recv_g, along_z(i))

    for i in Z_ORDER:
        chunk_z(i).start()
        gram_z(i).start()

    def chunk_plane(i, k):
        at = lax.rem(z + 8 - i, 8)
        return remote(chunks.at[at, s], chunks.at[at, s], send_c, recv_c.at[i], plane(k))

    @pl.loop(1, 16)
    def _(k):
        chunk_plane(0, k).start()

    for n, i in enumerate(Z_ORDER):
        chunk_z(i).wait_recv()

        @pl.loop(1, 16)
        def _(k):
            chunk_plane(i, k).start()

        if n == 2:
            pass
    drain(gy_z.at[pl.ds(0, 7)], recv_g)
    gy_all[s] = jnp.concatenate(
        [jnp.concatenate([gy_z[i, 0:1] for i in range(8)], axis=0), jnp.concatenate([gy_z[i, 1:2] for i in range(8)], axis=0)],
        axis=1,
    )

    def gram_plane(k):
        return remote(gy_all.at[s], gy_all.at[s], send_h, recv_h, plane(k))

    @pl.loop(1, 16)
    def _(k):
        gram_plane(k).start()

    in_noise.wait()
    in_steps.wait()
    zero_half = jnp.zeros((64, 64), F32)
    state[...] = jnp.concatenate([noise_a[...], zero_half], axis=1)
    which = assign[z]
    drain(gy_all.at[pl.ds(0, 15)], recv_h)
    for i in (0,) + Z_ORDER:
        drain(chunks.at[0, pl.ds(0, 15)], recv_c.at[i])
    gy = gy_all[...].reshape(128, 256)
    gy_high, gy_low = split(gy)
    lane = iota((64, 128), 1)
    chosen = jnp.where(lane == 64 + which, 1.0, 0.0)

    @pl.loop(0, STEPS)
    def _(k):
        now = 1.0 - k.astype(F32) * STEP
        latent = state[...]
        rounded = latent.astype(BF16).astype(F32)
        x = rounded + chosen
        x16 = x.astype(BF16)
        x_time = (x + jnp.where(lane == 96, now, 0.0)).astype(BF16)
        mixed = dot(x_time, gy_high) + dot(x_time, gy_low)
        second = jnp.where(lane == TIME_ROW - 128, now, 0.0)
        variance = jnp.sum(mixed[:, :128] * x + mixed[:, 128:] * second, axis=1, keepdims=True)
        inv = lax.rsqrt(jnp.maximum(variance, 0.0) + EPSILON)
        skip = jnp.concatenate([mixed[:, 96:160], zero_half], axis=1)
        moved = None
        for zi in range(8):
            weights = chunks[zi].reshape(512, 128)
            up = jnp.concatenate([weights[160 * t : 160 * t + 128] for t in range(3)], axis=1)
            down = jnp.concatenate([weights[160 * t + 96 : 160 * t + 160] for t in range(3)], axis=1)
            timed = weights[480:496].astype(F32)
            bias = jnp.concatenate([timed[t : t + 1] for t in range(3)], axis=1) * now
            hidden = (dot(x16, up) + bias) * inv
            act = jax.nn.gelu(hidden, approximate=True).astype(BF16)
            product = dot_t(act, down)
            moved = product if moved is None else moved + product
        moved = jnp.concatenate([moved, zero_half], axis=1).astype(BF16)
        vel_out[k] = moved
        swap = remote(vel_out.at[k], vel_in.at[k], send_v.at[k], recv_v.at[k], other_core)
        swap.start()
        fresh = jnp.concatenate([noise_b[k], zero_half], axis=1)
        partly = latent - STEP * skip + NOISE_GAIN * fresh
        swap.wait_recv()
        state[...] = partly - STEP * (moved.astype(F32) + vel_in[k].astype(F32))

    latent = state[...][:, :64]
    image = (latent * LATENT_SCALE).astype(BF16)
    image32 = image.astype(F32)
    empty = jnp.zeros((1, 64), F32)
    before = jnp.concatenate([empty, image32[:63]], axis=0)
    after = jnp.concatenate([image32[1:], empty], axis=0)
    wide = jnp.concatenate([before, image32, after], axis=1).astype(BF16)
    conv = dot(wide, w_tok[...])
    sums4 = jnp.sum(conv, axis=0, keepdims=True)
    channel_mean = sum(sums4[:, VC * i : VC * i + VC] for i in range(4)) / 256.0
    away = conv - jnp.concatenate([channel_mean] * 4, axis=1)
    squares4 = jnp.sum(away * away, axis=0, keepdims=True)
    channel_var = sum(squares4[:, VC * i : VC * i + VC] for i in range(4)) / 256.0
    stack = jnp.concatenate(
        [channel_mean, channel_var, channel_mean * channel_mean, jnp.zeros((5, VC), F32)], axis=0
    )
    member = jnp.where((iota((VC, 128), 0) >> 4) == (iota((VC, 128), 1) & 31), 1.0, 0.0)
    grouped = dot(stack, member, precision=HIGH) / 16.0
    average = grouped[0:1]
    variance = grouped[1:2] + jnp.maximum(grouped[2:3] - average * average, 0.0)
    inv = lax.rsqrt(variance + EPSILON)
    mean_high, mean_low = split(average)
    inv_high, inv_low = split(inv)
    lane1 = iota((1, 128), 1)
    stats = jnp.where(
        lane1 < 32,
        mean_high.astype(F32),
        jnp.where(lane1 < 64, mean_low.astype(F32), jnp.where(lane1 < 96, inv_high.astype(F32), inv_low.astype(F32))),
    )
    pair, token = iota((64, 64), 0), iota((64, 64), 1)
    pairs = jnp.concatenate(
        [dot(onehot(token == 2 * pair - 1), image), dot(onehot(token == 2 * pair), image)], axis=1
    ).astype(BF16)
    row, col = iota((64, 64), 0), iota((64, 64), 1)
    place = row & 7
    wanted = jnp.logical_and(place < 3, col == 4 * (row >> 3) + 2 * c + place)
    sent = dot(onehot(wanted), pairs) + jnp.where((iota((64, 128), 0) & 7) == 3, stats, 0.0)
    tile_out[...] = sent.reshape(8, 8, 128)
    tile_z[z] = tile_out[z]

    def tile_to(i):
        to = lax.rem(z + i, 8)
        return remote(tile_out.at[to], tile_z.at[z], send_t, recv_t, (s, to * 2 + c))

    for i in Z_ORDER:
        tile_to(i).start()
    lat_out[...] = jnp.concatenate([latent[:32], latent[32:]], axis=1)
    lat_in[z] = lat_out[...]

    def latent_to(i):
        return remote(lat_out, lat_in.at[z], send_l, recv_l, along_z(i))

    for i in Z_ORDER:
        latent_to(i).start()
    drain(tile_z.at[pl.ds(0, 7)], recv_t)
    row, col = iota((32, 64), 0), iota((32, 64), 1)
    tile_pack[...] = dot(
        onehot(col == 8 * (row >> 2) + (row & 3)), tile_z[...].reshape(64, 128).astype(BF16)
    ).astype(BF16)
    tiles[s] = tile_pack[...]

    def tile_plane(k):
        return remote(tile_pack, tiles.at[s], send_u, recv_u, plane(k))

    @pl.loop(1, 16)
    def _(k):
        tile_plane(k).start()

    spread = onehot((iota((128, 512), 1) >> 2) == iota((128, 512), 0))
    slots = jnp.broadcast_to(slot_map[...].astype(F32).reshape(1, 128), (8, 128)).astype(BF16)
    slot_of = dot(slots, spread)[0:1]
    row, col = iota((64, 512), 0), iota((64, 512), 1)
    here = (16 * s + (row & 15)).astype(F32)
    pick = onehot(jnp.logical_and(slot_of == here, (col & 3) == (row >> 4)))
    in_mid.wait()
    drain(tiles.at[pl.ds(0, 15)], recv_u)
    picked = dot(pick, tiles[...].reshape(512, 128))
    tokens = jnp.concatenate(
        [picked[16 * (i // 2) : 16 * (i // 2) + 16, 64 * (i % 2) : 64 * (i % 2) + 64] for i in range(6)], axis=0
    )
    none = jnp.zeros((16, 64), F32)
    wide = jnp.concatenate(
        [jnp.concatenate([none, tokens[:80]], axis=0), tokens, jnp.concatenate([tokens[16:], none], axis=0)], axis=1
    ).astype(BF16)
    conv = dot(wide, w_tok[...])
    line, channel = iota((128, 1024), 0), iota((128, 1024), 1)
    widen = onehot(
        jnp.logical_and((line & 31) == ((channel & 511) >> 4), (line >= 64) == (channel >= 512))
    )
    wide_stats = dot(picked[48:64].astype(BF16), widen)
    average, inv = wide_stats[:, :VC], wide_stats[:, VC:]
    strength = inv * gn_gain[...].reshape(1, VC)
    left = jnp.where(m == 0, 0.0, 1.0)
    right = jnp.where(m == 15, 0.0, 1.0)
    for row, act in ((0, act0), (1, act1)):
        for at in range(10):
            token, half = (at + 1) // 2, (at + 1) % 2
            here = VC * (2 * row + half)
            shaped = (conv[16 * token : 16 * token + 16, here : here + VC] - average) * strength
            value = jax.nn.silu(shaped)
            if at == 0:
                value = value * left
            if at == 9:
                value = value * right
            act[16 * at : 16 * at + 16] = value.astype(BF16)
    order = onehot(
        iota((128, 128), 1) == (iota((128, 128), 0) & 7) * 16 + (iota((128, 128), 0) >> 3)
    )
    for row in range(2):
        total = jnp.concatenate(
            [
                conv[16 * (1 + at // 2) : 16 * (1 + at // 2) + 16, VC * (2 * row + at % 2) : VC * (2 * row + at % 2) + VC]
                for at in range(8)
            ],
            axis=0,
        )
        for tap in range(3):
            total = total + dot(act0[16 * tap : 16 * tap + 128], w_mid[1 - row, tap])
            total = total + dot(act1[16 * tap : 16 * tap + 128], w_mid[2 - row, tap])
        ordered = dot(order, total.astype(BF16)).astype(BF16)
        dec_ref[:, row] = ordered.reshape(16, 8, VC)

    drain(lat_in.at[pl.ds(0, 7)], recv_l)
    for i in range(8):
        lat_ref[64 * i : 64 * i + 32] = lat_in[i][:, :64]
        lat_ref[64 * i + 32 : 64 * i + 64] = lat_in[i][:, 64:]

    @pl.loop(0, 16)
    def _(i):
        @pl.when(jnp.logical_not(jnp.logical_and(on_diagonal, i == m)))
        def _():
            to_features(i).wait_send()

    drain(parts.at[pl.ds(0, 15)], send_r)
    drain(chunks.at[0, pl.ds(0, 7)], send_z)
    drain(gy_z.at[pl.ds(0, 7)], send_g)
    for _ in range(8):
        drain(chunks.at[0, pl.ds(0, 15)], send_c)
    drain(gy_all.at[pl.ds(0, 15)], send_h)

    @pl.loop(0, STEPS)
    def _(k):
        remote(vel_out.at[k], vel_in.at[k], send_v.at[k], recv_v.at[k], other_core).wait_send()

    drain(tile_z.at[pl.ds(0, 7)], send_t)
    drain(lat_in.at[pl.ds(0, 7)], send_l)
    drain(tiles.at[pl.ds(0, 15)], send_u)


def per_device(*args):
    vmem, anywhere, smem = (
        pl.BlockSpec(memory_space=pltpu.VMEM),
        pl.BlockSpec(memory_space=pl.ANY),
        pl.BlockSpec(memory_space=pltpu.SMEM),
    )
    noise0, noise_k, assign, slot_map, prompt, time_vec, w_in, gain, w_up, w_down, w_out, conv_in, gn_gain, conv_mid = args
    dma = pltpu.SemaphoreType.DMA
    return pl.pallas_call(
        kernel,
        out_shape=(jax.ShapeDtypeStruct((512, 64), F32), jax.ShapeDtypeStruct((16, 2, 8, VC), BF16)),
        in_specs=[smem, vmem, anywhere, anywhere] + [vmem] * 9 + [anywhere],
        out_specs=(vmem, vmem),
        scratch_shapes=[
            pltpu.VMEM((16, 128), BF16),
            pltpu.VMEM((16, 16, 128), BF16),
            pltpu.VMEM((256, 256), F32),
            pltpu.VMEM((16, 40, 128), F32),
            pltpu.VMEM((16, 40, 128), F32),
            pltpu.VMEM((8, 16, 32, 128), BF16),
            pltpu.VMEM((8, 128), F32),
            pltpu.VMEM((8, 8, 128), F32),
            pltpu.VMEM((16, 8, 256), F32),
            pltpu.VMEM((STEPS, 64, 128), BF16),
            pltpu.VMEM((STEPS, 64, 128), BF16),
            pltpu.VMEM((64, 128), F32),
            pltpu.VMEM((8, 8, 128), F32),
            pltpu.VMEM((8, 8, 128), F32),
            pltpu.VMEM((32, 128), BF16),
            pltpu.VMEM((16, 32, 128), BF16),
            pltpu.VMEM((32, 128), F32),
            pltpu.VMEM((8, 32, 128), F32),
            pltpu.VMEM((64, 64), F32),
            pltpu.VMEM((STEPS, 64, 64), F32),
            pltpu.VMEM((3, 3, VC, VC), BF16),
            pltpu.VMEM((192, 4 * VC), BF16),
            pltpu.VMEM((160, VC), BF16),
            pltpu.VMEM((160, VC), BF16),
            dma((3,)),
            dma, dma,
            dma, dma,
            dma, dma((8,)),
            dma, dma,
            dma, dma((8,)),
            dma, dma,
            dma((STEPS,)), dma((STEPS,)),
            dma, dma,
            dma, dma,
            dma, dma,
        ],
        compiler_params=pltpu.CompilerParams(collective_id=0, has_side_effects=True, vmem_limit_bytes=40 << 20),
        name="rollout",
    )(assign, slot_map, noise0, noise_k, prompt, time_vec, w_in, gain, w_up, w_down, w_out, conv_in, gn_gain, conv_mid)


def solution(mesh):
    return jax.shard_map(
        per_device,
        mesh=mesh,
        in_specs=(
            P("segment", None),
            P(None, "segment", None),
            P("segment"),
            P(),
            P("segment", "mp"),
            P("mp"),
            P("segment", "mp"),
            P("mp"),
            P("segment", "mp"),
            P("mp", "segment"),
            P("mp", "segment"),
            P(),
            P(),
            P(),
        ),
        out_specs=(P("segment", None), P("segment", None, "mp", None)),
        check_vma=False,
    )
```

time: 557 us -> 80.4 us (0.14)
  the two profiles are of different devices: /device:TPU:1 before, /device:TPU:32 now
where the time goes in v1:
time: 80.4 us; the launch traced here: 80 us
  Pallas kernels  64.9 us (81%)
  local copies, waits for them, and re-layouts  14.4 us (18%)
    pallas_call x1, Pallas kernels, per_device(): pl.pallas_call(kernel, out_shape=(jax.ShapeDtypeStruct((512, 64), F32), j...  64.9 us
    unnamed x25, local copies, waits for them, and re-layouts  13.7 us

profile of v1, /device:TPU:32, one launch (start us, length us, event | category | flops | bytes accessed | tf_op | source)
XLA Modules:
  0.0 80.0 jit_solution(17122726637047433774)
XLA Ops:
  0.6 0.8 copy.19.w_out
  1.4 1.0 %copy.18.w_down = bf16[384,96]{1,0:T(8,128)(2,1)S(1)} copy(bf16[384,96]{0,1:T(8,128)(2,1)} %param.23) | data formatting | bytes 147456 | tf_op args[9]
  2.4 1.0 %copy.16.noise0 = f32[512,64]{1,0:T(8,128)S(1)} copy(f32[512,64]{0,1:T(8,128)} %param.14) | data formatting | bytes 262144 | tf_op args[0]
  3.5 1.4 %copy.17.noise_k = f32[4,512,64]{2,1,0:T(8,128)S(1)} copy(f32[4,512,64]{1,2,0:T(8,128)} %param.15) | data formatting | bytes 1048576 | tf_op args[1]
  4.8 0.0 copy-start
  4.9 2.3 %copy-done = bf16[3,3,512,512]{3,2,1,0:T(8,128)(2,1)S(1)} copy-done((bf16[3,3,512,512]{3,2,1,0:T(8,128)(2,1)S(1)}, bf16[3,3,512,512]{3,2,1,0:T(8,128)(2,1)}, u32[]{:S(2)}) %copy-start) | copy-done | bytes 4718616
  7.2 0.0 copy-start.1
  7.2 0.9 %copy-done.1 = bf16[3,3,16,512]{3,2,1,0:T(8,128)(2,1)S(1)} copy-done((bf16[3,3,16,512]{3,2,1,0:T(8,128)(2,1)S(1)}, bf16[3,3,16,512]{3,2,1,0:T(8,128)(2,1)}, u32[]{:S(2)}) %copy-start.1) | copy-done | bytes 147480
  8.1 0.0 copy-start.2
  8.1 0.9 %copy-done.2 = bf16[96,384]{1,0:T(8,128)(2,1)S(1)} copy-done((bf16[96,384]{1,0:T(8,128)(2,1)S(1)}, bf16[96,384]{1,0:T(8,128)(2,1)}, u32[]{:S(2)}) %copy-start.2) | copy-done | bytes 73752
  9.0 0.0 copy-start.3
  9.0 0.7 copy-done.3
  9.7 0.0 copy-start.4
  9.7 0.7 copy-done.4
  10.3 0.0 copy-start.5
  10.4 0.7 copy-done.5
  11.0 0.0 copy-start.6
  11.0 0.7 copy-done.6
  11.7 0.0 copy-start.7
  11.7 0.7 copy-done.7
  12.3 0.0 copy-start.8
  12.3 0.7 copy-done.8
  13.0 0.0 copy-start.9
  13.0 0.7 copy-done.9
  13.6 64.9 %rollout.1 = (f32[512,64]{1,0:T(8,128)S(1)}, bf16[16,2,8,512]{3,2,1,0:T(8,128)(2,1)S(1)}) custom-call(s32[8]{0:T(128)S(1)} %copy-done.5, s32[128]{0:T(128)S(1)} %copy-done.6, f32[512,64]{1,0:T(8,128)S(1)} %copy.16.noise0, f32[4,512,64]{2,1,0:T(8,128)S(1)} %copy.17.noise_k, bf16[2,96]{1,0:T(2,128)(2,1)S(1)} %copy-done.7, bf16[96]{0:T(256)(128)(2,1)S(1)} %copy-done.8, ...), custom_call_target="tpu_custom_call" | custom-call | tf_op jit(solution)/shard_map/rollout/pallas_call | solution.py:479
  78.5 0.8 copy.20
  79.3 0.7 copy.22
Async XLA Ops:
  4.8 2.3 %copy-start = (bf16[3,3,512,512]{3,2,1,0:T(8,128)(2,1)S(1)}, bf16[3,3,512,512]{3,2,1,0:T(8,128)(2,1)}, u32[]{:S(2)}) copy-start(bf16[3,3,512,512]{3,2,1,0:T(8,128)(2,1)} %conv_mid.1) | copy-start | bytes 14155780
  7.2 0.9 %copy-start.1 = (bf16[3,3,16,512]{3,2,1,0:T(8,128)(2,1)S(1)}, bf16[3,3,16,512]{3,2,1,0:T(8,128)(2,1)}, u32[]{:S(2)}) copy-start(bf16[3,3,16,512]{3,2,1,0:T(8,128)(2,1)} %conv_in.1) | copy-start | bytes 442372
  8.1 0.9 %copy-start.2 = (bf16[96,384]{1,0:T(8,128)(2,1)S(1)}, bf16[96,384]{1,0:T(8,128)(2,1)}, u32[]{:S(2)}) copy-start(bf16[96,384]{1,0:T(8,128)(2,1)} %w_up.1) | copy-start | bytes 221188
  9.0 0.7 copy-start.3
  9.7 0.7 copy-start.4
  10.3 0.7 copy-start.5
  11.0 0.7 copy-start.6
  11.7 0.7 copy-start.7
  12.3 0.7 copy-start.8
  13.0 0.7 copy-start.9

commit v2 on v1

--- a/solution.py
+++ b/solution.py
@@ -39,12 +39,14 @@
 
 
 def kernel(
-    assign, slot_map, noise0, noise_k, prompt, time_vec, w_in, gain, w_up, w_down, w_out, conv_in, gn_gain, conv_mid,
+    assign_in, slot_in, noise0, noise_k, prompt_in, time_in, w_in_in, gain_in, w_up_in, w_down_in, w_out_in, conv_in_in,
+    gn_in, conv_mid,
     lat_ref, dec_ref,
-    piece, tables, gram, part, parts, chunks, gy_own, gy_z, gy_all, vel_out, vel_in, state,
-    tile_out, tile_z, tile_pack, tiles, lat_out, lat_in, noise_a, noise_b, w_mid, w_tok, act0, act1,
-    in_sem, send_p, recv_p, send_r, recv_r, send_z, recv_z, send_g, recv_g, send_c, recv_c, send_h, recv_h,
-    send_v, recv_v, send_t, recv_t, send_u, recv_u, send_l, recv_l,
+    assign, slot_map, prompt, time_vec, w_in, gain, w_up, w_down, w_out, conv_in, gn_gain,
+    piece, tables, gram, part, parts, chunks, gy_own, gy_z, gy_all, gy_halves, vel_out, vel_in, state,
+    tile_out, tile_z, tile_pack, tiles, lat_out, lat_in, noise_a, noise_b, noise_t, w_mid, w_tok, act0, act1,
+    in_sem, send_p, recv_p, send_r, recv_r, send_z, recv_z, send_g, recv_g, send_c, recv_c, send_f, recv_f, send_h, recv_h, send_v, recv_v,
+    send_t, recv_t, send_u, recv_u, send_l, recv_l,
 ):
     s, m = lax.axis_index("segment"), lax.axis_index("mp")
     z, c = lax.div(m, 2), lax.rem(m, 2)
@@ -65,6 +67,28 @@
 
     def drain(ref, sem):
         pltpu.make_async_copy(ref, ref, sem).wait()
+
+    lanes = pl.ds(pl.multiple_of(lax.div(z, 2) * 128, 128), 128)
+    early = [
+        pltpu.make_async_copy(src, dst, in_sem.at[3 + n])
+        for n, (src, dst) in enumerate(
+            [(w_in_in, w_in), (prompt_in, prompt), (time_in, time_vec), (gain_in, gain), (w_out_in, w_out)]
+        )
+    ]
+    in_conv = pltpu.make_async_copy(conv_in_in, conv_in, in_sem.at[8])
+    later = [
+        pltpu.make_async_copy(src, dst, in_sem.at[9 + n])
+        for n, (src, dst) in enumerate([(w_up_in, w_up), (w_down_in, w_down)])
+    ]
+    last = [
+        pltpu.make_async_copy(src, dst, in_sem.at[11 + n])
+        for n, (src, dst) in enumerate([(assign_in, assign), (slot_in, slot_map), (gn_in, gn_gain)])
+    ]
+    in_noise = pltpu.make_async_copy(noise0.at[:, lanes], noise_a, in_sem.at[0])
+    in_steps = pltpu.make_async_copy(noise_k.at[:, :, lanes], noise_b, in_sem.at[1])
+    in_mid = pltpu.make_async_copy(conv_mid, w_mid, in_sem.at[2])
+    for copy in early + later + [in_conv, in_noise, in_steps] + last + [in_mid]:
+        copy.start()
 
     barrier = pltpu.get_barrier_semaphore()
 
@@ -87,23 +111,17 @@
 
     greet(other_core)
 
-    rows = pl.ds(pl.multiple_of(z * 64, 64), 64)
-    in_noise = pltpu.make_async_copy(noise0.at[rows], noise_a, in_sem.at[0])
-    in_steps = pltpu.make_async_copy(noise_k.at[:, rows], noise_b, in_sem.at[1])
-    in_mid = pltpu.make_async_copy(conv_mid, w_mid, in_sem.at[2])
-    in_noise.start()
-    in_steps.start()
-    in_mid.start()
+    for copy in early:
+        copy.wait()
 
     first = jnp.where(s == 0, 1.0, 0.0)
-    turned = dot_t(onehot(iota((4, 4), 0) == iota((4, 4), 1)), w_out[...])
     block = jnp.concatenate(
         [
             w_in[...].astype(F32),
             prompt[...].astype(F32),
             time_vec[...].astype(F32).reshape(1, 96) * first,
             jnp.ones((1, 96), F32),
-            turned,
+            w_out[...].astype(F32),
             gain[...].astype(F32).reshape(1, 96),
             jnp.zeros((3, 96), F32),
         ],
@@ -126,6 +144,7 @@
         def _():
             to_features(i).start()
 
+    in_conv.wait()
     w_tok[...] = jnp.zeros(w_tok.shape, BF16)
     for row in range(2):
         for col in range(2):
@@ -135,6 +154,12 @@
                     to = (offset // 2) * 64 + (2 * src_row + offset % 2) * 16
                     at = (2 * row + col) * VC
                     w_tok[to : to + 16, at : at + VC] = conv_in[src_row - row + 1, tap]
+
+    for copy in later + [in_noise, in_steps] + last:
+        copy.wait()
+    noise_t[0] = noise_a[...].T
+    for k in range(STEPS):
+        noise_t[1 + k] = noise_b[k].T
 
     @pl.when(on_diagonal)
     def _():
@@ -164,7 +189,7 @@
     table16 = table.astype(BF16)
     scaled_high, scaled_low = split(table * table[GAIN_ROW : GAIN_ROW + 1])
     up_part = dot(scaled_high[:, :96], w_up[...]) + dot(scaled_low[:, :96], w_up[...])
-    down_part = dot_t(table16[96:160, :96], w_down[...])
+    down_part = dot(table16[96:160, :96], w_down[...])
     gram[...] = dot_t(table16, table16)
     for third in range(3):
         lanes = slice(128 * third, 128 * third + 128)
@@ -222,7 +247,7 @@
         else:
             time_rows = jnp.zeros((16, 128), F32)
         taken = jnp.where(s == 15, time_rows, column * row)
-        chunks[z, s, 16 * half : 16 * half + 16] = (block - taken).astype(BF16)
+        chunks[c, z, s, 16 * half : 16 * half + 16] = (block - taken).astype(BF16)
     own = jnp.concatenate([total[37:38], total[38:39]], axis=1)
     own_index = 8 * s + z
     own_lane = own_index + jnp.where(own_index >= 96, 64, 0)
@@ -234,90 +259,110 @@
     gy_z[z] = gy_own[...]
 
     def chunk_z(i):
-        return remote(chunks.at[z, s], chunks.at[z, s], send_z, recv_z.at[i], along_z(i))
+        block = chunks.at[c, z, s]
+        return remote(block, block, send_z, recv_z.at[i], along_z(i))
 
     def gram_z(i):
         return remote(gy_own, gy_z.at[z], send_g, recv_g, along_z(i))
 
     for i in Z_ORDER:
+        gram_z(i).start()
         chunk_z(i).start()
-        gram_z(i).start()
-
-    def chunk_plane(i, k):
-        at = lax.rem(z + 8 - i, 8)
-        return remote(chunks.at[at, s], chunks.at[at, s], send_c, recv_c.at[i], plane(k))
-
-    @pl.loop(1, 16)
-    def _(k):
-        chunk_plane(0, k).start()
-
-    for n, i in enumerate(Z_ORDER):
-        chunk_z(i).wait_recv()
+
+    def from_z(i):
+        return lax.rem(z + 8 - i, 8)
+
+    def spread(i):
+        block = chunks.at[c, from_z(i), s]
 
         @pl.loop(1, 16)
         def _(k):
-            chunk_plane(i, k).start()
-
-        if n == 2:
-            pass
-    drain(gy_z.at[pl.ds(0, 7)], recv_g)
-    gy_all[s] = jnp.concatenate(
-        [jnp.concatenate([gy_z[i, 0:1] for i in range(8)], axis=0), jnp.concatenate([gy_z[i, 1:2] for i in range(8)], axis=0)],
-        axis=1,
-    )
+            remote(block, block, send_c, recv_c.at[i], plane(k)).start()
+
+    def to_core(i):
+        block = chunks.at[c, from_z(i)]
+        return remote(block, block, send_f, recv_f.at[i], other_core)
 
     def gram_plane(k):
         return remote(gy_all.at[s], gy_all.at[s], send_h, recv_h, plane(k))
 
-    @pl.loop(1, 16)
-    def _(k):
-        gram_plane(k).start()
-
-    in_noise.wait()
-    in_steps.wait()
+    order = (0,) + Z_ORDER
+    for n, i in enumerate(order):
+        if n:
+            chunk_z(i).wait_recv()
+        if n == 7:
+            drain(gy_z.at[pl.ds(0, 7)], recv_g)
+            gy_all[s] = jnp.concatenate(
+                [jnp.concatenate([gy_z[j, row : row + 1] for j in range(8)], axis=0) for row in range(2)], axis=1
+            )
+
+            @pl.loop(1, 16)
+            def _(k):
+                gram_plane(k).start()
+
+        spread(i)
+
+    own_half = pl.ds(pl.multiple_of(lax.rem(z, 2) * 64, 64), 64)
     zero_half = jnp.zeros((64, 64), F32)
-    state[...] = jnp.concatenate([noise_a[...], zero_half], axis=1)
+    state[...] = jnp.concatenate([noise_t[0, own_half], zero_half], axis=1)
     which = assign[z]
-    drain(gy_all.at[pl.ds(0, 15)], recv_h)
-    for i in (0,) + Z_ORDER:
-        drain(chunks.at[0, pl.ds(0, 15)], recv_c.at[i])
-    gy = gy_all[...].reshape(128, 256)
-    gy_high, gy_low = split(gy)
     lane = iota((64, 128), 1)
     chosen = jnp.where(lane == 64 + which, 1.0, 0.0)
 
-    @pl.loop(0, STEPS)
+    def before_layer(now):
+        latent = state[...]
+        rows = latent.astype(BF16).astype(F32) + chosen
+        rows_time = (rows + jnp.where(lane == 96, now, 0.0)).astype(BF16)
+        mixed = dot(rows_time, gy_halves[0]) + dot(rows_time, gy_halves[1])
+        second = jnp.where(lane == TIME_ROW - 128, now, 0.0)
+        variance = jnp.sum(mixed[:, :128] * rows + mixed[:, 128:] * second, axis=1, keepdims=True)
+        inv = lax.rsqrt(jnp.maximum(variance, 0.0) + EPSILON)
+        return latent, rows.astype(BF16), inv, mixed[:, 96:160]
+
+    def layer(core, group, rows16, inv, now):
+        weights = [chunks[core, from_z(i)].reshape(512, 128) for i in group]
+        up = jnp.concatenate([w[160 * t : 160 * t + 128] for w in weights for t in range(3)], axis=1)
+        down = jnp.concatenate([w[160 * t + 96 : 160 * t + 160] for w in weights for t in range(3)], axis=1)
+        timed = [w[480:496].astype(F32) for w in weights]
+        bias = jnp.concatenate([w[t : t + 1] for w in timed for t in range(3)], axis=1) * now
+        hidden = (dot(rows16, up) + bias) * inv
+        return dot_t(jax.nn.gelu(hidden, approximate=True).astype(BF16), down)
+
+    def after_layer(k, latent, moved, skip):
+        change = jnp.concatenate([moved + skip, zero_half], axis=1)
+        fresh = jnp.concatenate([noise_t[1 + k, own_half], zero_half], axis=1)
+        state[...] = latent - STEP * change + NOISE_GAIN * fresh
+
+    groups = (order[:4], order[4:])
+
+    def arrived(group):
+        for i in group:
+            drain(chunks.at[c, 0, pl.ds(0, 15)], recv_c.at[i])
+            to_core(i).start()
+
+    arrived(groups[0])
+    drain(gy_all.at[pl.ds(0, 15)], recv_h)
+    gy_high, gy_low = split(gy_all[...].reshape(128, 256))
+    gy_halves[0] = gy_high
+    gy_halves[1] = gy_low
+    latent, rows16, inv, skip = before_layer(1.0)
+    moved = layer(c, groups[0], rows16, inv, 1.0)
+    arrived(groups[1])
+    moved = moved + layer(c, groups[1], rows16, inv, 1.0)
+    vel_out[...] = jnp.concatenate([moved, moved], axis=1).astype(BF16)
+    swap = remote(vel_out, vel_in, send_v, recv_v, other_core)
+    swap.start()
+    swap.wait_recv()
+    after_layer(0, latent, (vel_out[...].astype(F32) + vel_in[...].astype(F32))[:, :64], skip)
+    for i in order:
+        drain(chunks.at[c, 0], recv_f.at[i])
+
+    @pl.loop(1, STEPS)
     def _(k):
         now = 1.0 - k.astype(F32) * STEP
-        latent = state[...]
-        rounded = latent.astype(BF16).astype(F32)
-        x = rounded + chosen
-        x16 = x.astype(BF16)
-        x_time = (x + jnp.where(lane == 96, now, 0.0)).astype(BF16)
-        mixed = dot(x_time, gy_high) + dot(x_time, gy_low)
-        second = jnp.where(lane == TIME_ROW - 128, now, 0.0)
-        variance = jnp.sum(mixed[:, :128] * x + mixed[:, 128:] * second, axis=1, keepdims=True)
-        inv = lax.rsqrt(jnp.maximum(variance, 0.0) + EPSILON)
-        skip = jnp.concatenate([mixed[:, 96:160], zero_half], axis=1)
-        moved = None
-        for zi in range(8):
-            weights = chunks[zi].reshape(512, 128)
-            up = jnp.concatenate([weights[160 * t : 160 * t + 128] for t in range(3)], axis=1)
-            down = jnp.concatenate([weights[160 * t + 96 : 160 * t + 160] for t in range(3)], axis=1)
-            timed = weights[480:496].astype(F32)
-            bias = jnp.concatenate([timed[t : t + 1] for t in range(3)], axis=1) * now
-            hidden = (dot(x16, up) + bias) * inv
-            act = jax.nn.gelu(hidden, approximate=True).astype(BF16)
-            product = dot_t(act, down)
-            moved = product if moved is None else moved + product
-        moved = jnp.concatenate([moved, zero_half], axis=1).astype(BF16)
-        vel_out[k] = moved
-        swap = remote(vel_out.at[k], vel_in.at[k], send_v.at[k], recv_v.at[k], other_core)
-        swap.start()
-        fresh = jnp.concatenate([noise_b[k], zero_half], axis=1)
-        partly = latent - STEP * skip + NOISE_GAIN * fresh
-        swap.wait_recv()
-        state[...] = partly - STEP * (moved.astype(F32) + vel_in[k].astype(F32))
+        latent, rows16, inv, skip = before_layer(now)
+        half = [layer(core, groups[0], rows16, inv, now) + layer(core, groups[1], rows16, inv, now) for core in range(2)]
+        after_layer(k, latent, half[0] + half[1], skip)
 
     latent = state[...][:, :64]
     image = (latent * LATENT_SCALE).astype(BF16)
@@ -424,7 +469,7 @@
             if at == 9:
                 value = value * right
             act[16 * at : 16 * at + 16] = value.astype(BF16)
-    order = onehot(
+    ordering = onehot(
         iota((128, 128), 1) == (iota((128, 128), 0) & 7) * 16 + (iota((128, 128), 0) >> 3)
     )
     for row in range(2):
@@ -438,13 +483,15 @@
         for tap in range(3):
             total = total + dot(act0[16 * tap : 16 * tap + 128], w_mid[1 - row, tap])
             total = total + dot(act1[16 * tap : 16 * tap + 128], w_mid[2 - row, tap])
-        ordered = dot(order, total.astype(BF16)).astype(BF16)
+        ordered = dot(ordering, total.astype(BF16)).astype(BF16)
         dec_ref[:, row] = ordered.reshape(16, 8, VC)
 
     drain(lat_in.at[pl.ds(0, 7)], recv_l)
-    for i in range(8):
-        lat_ref[64 * i : 64 * i + 32] = lat_in[i][:, :64]
-        lat_ref[64 * i + 32 : 64 * i + 64] = lat_in[i][:, 64:]
+    for i in range(4):
+        both = jnp.concatenate(
+            [half for pack in (lat_in[2 * i], lat_in[2 * i + 1]) for half in (pack[:, :64], pack[:, 64:])], axis=0
+        )
+        lat_ref[:, 128 * i : 128 * i + 128] = both.T
 
     @pl.loop(0, 16)
     def _(i):
@@ -453,46 +500,51 @@
             to_features(i).wait_send()
 
     drain(parts.at[pl.ds(0, 15)], send_r)
-    drain(chunks.at[0, pl.ds(0, 7)], send_z)
+    drain(chunks.at[c, 0, pl.ds(0, 7)], send_z)
     drain(gy_z.at[pl.ds(0, 7)], send_g)
     for _ in range(8):
-        drain(chunks.at[0, pl.ds(0, 15)], send_c)
+        drain(chunks.at[c, 0, pl.ds(0, 15)], send_c)
+        drain(chunks.at[c, 0], send_f)
     drain(gy_all.at[pl.ds(0, 15)], send_h)
-
-    @pl.loop(0, STEPS)
-    def _(k):
-        remote(vel_out.at[k], vel_in.at[k], send_v.at[k], recv_v.at[k], other_core).wait_send()
-
+    swap.wait_send()
     drain(tile_z.at[pl.ds(0, 7)], send_t)
     drain(lat_in.at[pl.ds(0, 7)], send_l)
     drain(tiles.at[pl.ds(0, 15)], send_u)
 
 
 def per_device(*args):
-    vmem, anywhere, smem = (
-        pl.BlockSpec(memory_space=pltpu.VMEM),
-        pl.BlockSpec(memory_space=pl.ANY),
-        pl.BlockSpec(memory_space=pltpu.SMEM),
-    )
+    vmem, anywhere = pl.BlockSpec(memory_space=pltpu.VMEM), pl.BlockSpec(memory_space=pl.ANY)
     noise0, noise_k, assign, slot_map, prompt, time_vec, w_in, gain, w_up, w_down, w_out, conv_in, gn_gain, conv_mid = args
     dma = pltpu.SemaphoreType.DMA
-    return pl.pallas_call(
+    latents, decoded = pl.pallas_call(
         kernel,
-        out_shape=(jax.ShapeDtypeStruct((512, 64), F32), jax.ShapeDtypeStruct((16, 2, 8, VC), BF16)),
-        in_specs=[smem, vmem, anywhere, anywhere] + [vmem] * 9 + [anywhere],
+        out_shape=(jax.ShapeDtypeStruct((64, 512), F32), jax.ShapeDtypeStruct((16, 2, 8, VC), BF16)),
+        in_specs=[anywhere] * 14,
         out_specs=(vmem, vmem),
         scratch_shapes=[
+            pltpu.SMEM((8,), jnp.int32),
+            pltpu.VMEM((128,), jnp.int32),
+            pltpu.VMEM((2, 96), BF16),
+            pltpu.VMEM((96,), BF16),
+            pltpu.VMEM((4, 96), BF16),
+            pltpu.VMEM((96,), BF16),
+            pltpu.VMEM((96, 384), BF16),
+            pltpu.VMEM((96, 384), BF16),
+            pltpu.VMEM((4, 96), BF16),
+            pltpu.VMEM((3, 3, 16, VC), BF16),
+            pltpu.VMEM((VC,), F32),
             pltpu.VMEM((16, 128), BF16),
             pltpu.VMEM((16, 16, 128), BF16),
             pltpu.VMEM((256, 256), F32),
             pltpu.VMEM((16, 40, 128), F32),
             pltpu.VMEM((16, 40, 128), F32),
-            pltpu.VMEM((8, 16, 32, 128), BF16),
+            pltpu.VMEM((2, 8, 16, 32, 128), BF16),
             pltpu.VMEM((8, 128), F32),
             pltpu.VMEM((8, 8, 128), F32),
             pltpu.VMEM((16, 8, 256), F32),
-            pltpu.VMEM((STEPS, 64, 128), BF16),
-            pltpu.VMEM((STEPS, 64, 128), BF16),
+            pltpu.VMEM((2, 128, 256), BF16),
+            pltpu.VMEM((64, 128), BF16),
+            pltpu.VMEM((64, 128), BF16),
             pltpu.VMEM((64, 128), F32),
             pltpu.VMEM((8, 8, 128), F32),
             pltpu.VMEM((8, 8, 128), F32),
@@ -500,27 +552,33 @@
             pltpu.VMEM((16, 32, 128), BF16),
             pltpu.VMEM((32, 128), F32),
             pltpu.VMEM((8, 32, 128), F32),
-            pltpu.VMEM((64, 64), F32),
-            pltpu.VMEM((STEPS, 64, 64), F32),
+            pltpu.VMEM((64, 128), F32),
+            pltpu.VMEM((STEPS, 64, 128), F32),
+            pltpu.VMEM((1 + STEPS, 128, 64), F32),
             pltpu.VMEM((3, 3, VC, VC), BF16),
             pltpu.VMEM((192, 4 * VC), BF16),
             pltpu.VMEM((160, VC), BF16),
             pltpu.VMEM((160, VC), BF16),
-            dma((3,)),
+            dma((14,)),
             dma, dma,
             dma, dma,
             dma, dma((8,)),
             dma, dma,
             dma, dma((8,)),
-            dma, dma,
-            dma((STEPS,)), dma((STEPS,)),
+            dma, dma((8,)),
+            dma, dma,
+            dma, dma,
             dma, dma,
             dma, dma,
             dma, dma,
         ],
-        compiler_params=pltpu.CompilerParams(collective_id=0, has_side_effects=True, vmem_limit_bytes=40 << 20),
+        compiler_params=pltpu.CompilerParams(collective_id=0, has_side_effects=True, vmem_limit_bytes=62 << 20),
         name="rollout",
-    )(assign, slot_map, noise0, noise_k, prompt, time_vec, w_in, gain, w_up, w_down, w_out, conv_in, gn_gain, conv_mid)
+    )(
+        assign, slot_map, noise0.T, noise_k.transpose(0, 2, 1), prompt, time_vec, w_in, gain, w_up, w_down.T, w_out.T,
+        conv_in, gn_gain, conv_mid,
+    )
+    return latents.T, decoded
 
 
 def solution(mesh):

time: 80.4 us -> 65.5 us (0.81)
  the two profiles are of different devices: /device:TPU:32 before, /device:TPU:1 now
where the time goes in v2:
time: 65.5 us; the launch traced here: 65.4 us
  Pallas kernels  61.5 us (94%)
  local copies, waits for them, and re-layouts  3.24 us (5%)
    pallas_call x1, Pallas kernels, per_device(): pl.pallas_call(kernel, out_shape=(jax.ShapeDtypeStruct((64, 512), F32), j...  61.5 us
    unnamed x2, local copies, waits for them, and re-layouts  3.24 us

profile of v2, /device:TPU:1, one launch (start us, length us, event | category | flops | bytes accessed | tf_op | source)
XLA Modules:
  0.0 65.4 jit_solution(1694510346617649913)
XLA Ops:
  0.6 61.5 %rollout.1 = (f32[64,512]{1,0:T(8,128)}, bf16[16,2,8,512]{3,2,1,0:T(8,128)(2,1)}) custom-call(s32[8]{0:T(128)} %assign_in.1, s32[128]{0:T(128)} %slot_in.1, f32[64,512]{1,0:T(8,128)} %bitcast.6, f32[4,64,512]{2,1,0:T(8,128)} %bitcast.5, bf16[2,96]{1,0:T(2,128)(2,1)} %prompt_in.1, bf16[96]{0:T(256)(128)(2,1)} %time_in.1, bf16[4,96]{1,0:T(4,128)(2,1)} %w_in_in.1, ...), custom_call_target="tpu_custom_call" | custom-call | tf_op jit(solution)/shard_map/rollout/pallas_call | solution.py:519
  62.2 1.6 %copy.18 = f32[512,64]{0,1:T(8,128)} copy(f32[512,64]{0,1:T(8,128)} %bitcast.7) | data formatting | bytes 262144
  63.7 1.7 %copy.19 = bf16[16,2,8,512]{3,2,1,0:T(8,128)(2,1)} copy(bf16[16,2,8,512]{3,2,1,0:T(8,128)(2,1)} %get-tuple-element.9) | data formatting | bytes 524288

commit v3 on v2

--- a/solution.py
+++ b/solution.py
@@ -67,6 +67,27 @@
 
     def drain(ref, sem):
         pltpu.make_async_copy(ref, ref, sem).wait()
+
+    barrier = pltpu.get_barrier_semaphore()
+
+    def greet(device):
+        pl.semaphore_signal(barrier, inc=1, device_id=device, device_id_type=MESH)
+
+    @pl.loop(0, 16)
+    def _(i):
+        @pl.when(jnp.logical_not(jnp.logical_and(on_diagonal, i == s)))
+        def _():
+            greet((i, s))
+
+    @pl.loop(1, 16)
+    def _(i):
+        greet(plane(i))
+
+    @pl.loop(1, 8)
+    def _(i):
+        greet(along_z(i))
+
+    greet(other_core)
 
     lanes = pl.ds(pl.multiple_of(lax.div(z, 2) * 128, 128), 128)
     early = [
@@ -89,27 +110,6 @@
     in_mid = pltpu.make_async_copy(conv_mid, w_mid, in_sem.at[2])
     for copy in early + later + [in_conv, in_noise, in_steps] + last + [in_mid]:
         copy.start()
-
-    barrier = pltpu.get_barrier_semaphore()
-
-    def greet(device):
-        pl.semaphore_signal(barrier, inc=1, device_id=device, device_id_type=MESH)
-
-    @pl.loop(0, 16)
-    def _(i):
-        @pl.when(jnp.logical_not(jnp.logical_and(on_diagonal, i == s)))
-        def _():
-            greet((i, s))
-
-    @pl.loop(1, 16)
-    def _(i):
-        greet(plane(i))
-
-    @pl.loop(1, 8)
-    def _(i):
-        greet(along_z(i))
-
-    greet(other_core)
 
     for copy in early:
         copy.wait()
@@ -438,6 +438,12 @@
     row, col = iota((64, 512), 0), iota((64, 512), 1)
     here = (16 * s + (row & 15)).astype(F32)
     pick = onehot(jnp.logical_and(slot_of == here, (col & 3) == (row >> 4)))
+    drain(lat_in.at[pl.ds(0, 7)], recv_l)
+    for i in range(4):
+        both = jnp.concatenate(
+            [half for pack in (lat_in[2 * i], lat_in[2 * i + 1]) for half in (pack[:, :64], pack[:, 64:])], axis=0
+        )
+        lat_ref[:, 128 * i : 128 * i + 128] = both.T
     in_mid.wait()
     drain(tiles.at[pl.ds(0, 15)], recv_u)
     picked = dot(pick, tiles[...].reshape(512, 128))
@@ -486,13 +492,6 @@
         ordered = dot(ordering, total.astype(BF16)).astype(BF16)
         dec_ref[:, row] = ordered.reshape(16, 8, VC)
 
-    drain(lat_in.at[pl.ds(0, 7)], recv_l)
-    for i in range(4):
-        both = jnp.concatenate(
-            [half for pack in (lat_in[2 * i], lat_in[2 * i + 1]) for half in (pack[:, :64], pack[:, 64:])], axis=0
-        )
-        lat_ref[:, 128 * i : 128 * i + 128] = both.T
-
     @pl.loop(0, 16)
     def _(i):
         @pl.when(jnp.logical_not(jnp.logical_and(on_diagonal, i == m)))
@@ -518,7 +517,7 @@
     dma = pltpu.SemaphoreType.DMA
     latents, decoded = pl.pallas_call(
         kernel,
-        out_shape=(jax.ShapeDtypeStruct((64, 512), F32), jax.ShapeDtypeStruct((16, 2, 8, VC), BF16)),
+        out_shape=(pltpu.VMEM((64, 512), F32), pltpu.VMEM((16, 2, 8, VC), BF16)),
         in_specs=[anywhere] * 14,
         out_specs=(vmem, vmem),
         scratch_shapes=[

time: 65.5 us -> 62.7 us (0.957)
  local copies, waits for them, and re-layouts: 3.24 us -> 1.36 us
  Pallas kernels: 61.5 us -> 60.6 us
    unnamed x2, local copies, waits for them, and re-layouts: 3.24 us -> 1.36 us
    pallas_call x1, Pallas kernels: 61.5 us -> 60.6 us  [per_device(): pl.pallas_call(kernel, out_shape=(pltpu.VMEM((64, 512), F32), pltpu.VMEM(...]
where the time goes in v3:
time: 62.7 us; the launch traced here: 62.6 us
  Pallas kernels  60.6 us (97%)
  local copies, waits for them, and re-layouts  1.36 us (2%)
  between operations  0.64 us (1%)
    pallas_call x1, Pallas kernels, per_device(): pl.pallas_call(kernel, out_shape=(pltpu.VMEM((64, 512), F32), pltpu.VMEM(...  60.6 us
    unnamed x2, local copies, waits for them, and re-layouts  1.36 us

profile of v3, /device:TPU:1, one launch (start us, length us, event | category | flops | bytes accessed | tf_op | source)
XLA Modules:
  0.0 62.6 jit_solution(1279418947551872224)
XLA Ops:
  0.6 60.6 %rollout.1 = (f32[64,512]{1,0:T(8,128)S(1)}, bf16[16,2,8,512]{3,2,1,0:T(8,128)(2,1)S(1)}) custom-call(s32[8]{0:T(128)} %assign_in.1, s32[128]{0:T(128)} %slot_in.1, f32[64,512]{1,0:T(8,128)} %bitcast.7, f32[4,64,512]{2,1,0:T(8,128)} %bitcast.6, bf16[2,96]{1,0:T(2,128)(2,1)} %prompt_in.1, bf16[96]{0:T(256)(128)(2,1)} %time_in.1, bf16[4,96]{1,0:T(4,128)(2,1)} %w_in_in.1, ...), custom_call_target="tpu_custom_call" | custom-call | tf_op jit(solution)/shard_map/rollout/pallas_call | solution.py:518
  61.2 0.7 %copy.18 = f32[512,64]{0,1:T(8,128)} copy(f32[512,64]{0,1:T(8,128)S(1)} %bitcast.5) | data formatting | bytes 262144
  61.9 0.7 %copy.19 = bf16[16,2,8,512]{3,2,1,0:T(8,128)(2,1)} copy(bf16[16,2,8,512]{3,2,1,0:T(8,128)(2,1)S(1)} %get-tuple-element.7) | data formatting | bytes 524288

commit v4 on v3

--- a/solution.py
+++ b/solution.py
@@ -44,7 +44,7 @@
     lat_ref, dec_ref,
     assign, slot_map, prompt, time_vec, w_in, gain, w_up, w_down, w_out, conv_in, gn_gain,
     piece, tables, gram, part, parts, chunks, gy_own, gy_z, gy_all, gy_halves, vel_out, vel_in, state,
-    tile_out, tile_z, tile_pack, tiles, lat_out, lat_in, noise_a, noise_b, noise_t, w_mid, w_tok, act0, act1,
+    tile_out, tile_z, tile_pack, tiles, lat_out, lat_in, noise_a, noise_b, noise_t, w_mid, w_tok, acts,
     in_sem, send_p, recv_p, send_r, recv_r, send_z, recv_z, send_g, recv_g, send_c, recv_c, send_f, recv_f, send_h, recv_h, send_v, recv_v,
     send_t, recv_t, send_u, recv_u, send_l, recv_l,
 ):
@@ -313,7 +313,7 @@
         latent = state[...]
         rows = latent.astype(BF16).astype(F32) + chosen
         rows_time = (rows + jnp.where(lane == 96, now, 0.0)).astype(BF16)
-        mixed = dot(rows_time, gy_halves[0]) + dot(rows_time, gy_halves[1])
+        mixed = dot(jnp.concatenate([rows_time, rows_time], axis=1), gy_halves[...].reshape(256, 256))
         second = jnp.where(lane == TIME_ROW - 128, now, 0.0)
         variance = jnp.sum(mixed[:, :128] * rows + mixed[:, 128:] * second, axis=1, keepdims=True)
         inv = lax.rsqrt(jnp.maximum(variance, 0.0) + EPSILON)
@@ -464,7 +464,7 @@
     strength = inv * gn_gain[...].reshape(1, VC)
     left = jnp.where(m == 0, 0.0, 1.0)
     right = jnp.where(m == 15, 0.0, 1.0)
-    for row, act in ((0, act0), (1, act1)):
+    for row in range(2):
         for at in range(10):
             token, half = (at + 1) // 2, (at + 1) % 2
             here = VC * (2 * row + half)
@@ -474,10 +474,11 @@
                 value = value * left
             if at == 9:
                 value = value * right
-            act[16 * at : 16 * at + 16] = value.astype(BF16)
+            acts[row, 16 * at : 16 * at + 16] = value.astype(BF16)
     ordering = onehot(
         iota((128, 128), 1) == (iota((128, 128), 0) & 7) * 16 + (iota((128, 128), 0) >> 3)
     )
+    same_row = sum(dot(acts[:, 16 * tap : 16 * tap + 128].reshape(256, VC), w_mid[1, tap]) for tap in range(3))
     for row in range(2):
         total = jnp.concatenate(
             [
@@ -486,9 +487,9 @@
             ],
             axis=0,
         )
+        total = total + same_row[128 * row : 128 * row + 128]
         for tap in range(3):
-            total = total + dot(act0[16 * tap : 16 * tap + 128], w_mid[1 - row, tap])
-            total = total + dot(act1[16 * tap : 16 * tap + 128], w_mid[2 - row, tap])
+            total = total + dot(acts[1 - row, 16 * tap : 16 * tap + 128], w_mid[2 - 2 * row, tap])
         ordered = dot(ordering, total.astype(BF16)).astype(BF16)
         dec_ref[:, row] = ordered.reshape(16, 8, VC)
 
@@ -556,8 +557,7 @@
             pltpu.VMEM((1 + STEPS, 128, 64), F32),
             pltpu.VMEM((3, 3, VC, VC), BF16),
             pltpu.VMEM((192, 4 * VC), BF16),
-            pltpu.VMEM((160, VC), BF16),
-            pltpu.VMEM((160, VC), BF16),
+            pltpu.VMEM((2, 160, VC), BF16),
             dma((14,)),
             dma, dma,
             dma, dma,

time: 62.7 us -> 62.6 us (level)
  no operation moved by 1% of the time
where the time goes in v4:
time: 62.6 us; the launch traced here: 62.5 us
  Pallas kernels  60.5 us (97%)
  local copies, waits for them, and re-layouts  1.36 us (2%)
  between operations  0.64 us (1%)
    pallas_call x1, Pallas kernels, per_device(): pl.pallas_call(kernel, out_shape=(pltpu.VMEM((64, 512), F32), pltpu.VMEM(...  60.5 us
    unnamed x2, local copies, waits for them, and re-layouts  1.36 us

profile of v4, /device:TPU:1, one launch (start us, length us, event | category | flops | bytes accessed | tf_op | source)
XLA Modules:
  0.0 62.5 jit_solution(15212563608849642980)
XLA Ops:
  0.6 60.5 %rollout.1 = (f32[64,512]{1,0:T(8,128)S(1)}, bf16[16,2,8,512]{3,2,1,0:T(8,128)(2,1)S(1)}) custom-call(s32[8]{0:T(128)} %assign_in.1, s32[128]{0:T(128)} %slot_in.1, f32[64,512]{1,0:T(8,128)} %bitcast.7, f32[4,64,512]{2,1,0:T(8,128)} %bitcast.6, bf16[2,96]{1,0:T(2,128)(2,1)} %prompt_in.1, bf16[96]{0:T(256)(128)(2,1)} %time_in.1, bf16[4,96]{1,0:T(4,128)(2,1)} %w_in_in.1, ...), custom_call_target="tpu_custom_call" | custom-call | tf_op jit(solution)/shard_map/rollout/pallas_call | solution.py:519
  61.2 0.7 %copy.18 = f32[512,64]{0,1:T(8,128)} copy(f32[512,64]{0,1:T(8,128)S(1)} %bitcast.5) | data formatting | bytes 262144
  61.8 0.7 %copy.19 = bf16[16,2,8,512]{3,2,1,0:T(8,128)(2,1)} copy(bf16[16,2,8,512]{3,2,1,0:T(8,128)(2,1)S(1)} %get-tuple-element.7) | data formatting | bytes 524288
